TPU v7x, 32 devices: a whole 2x2x4 slice. The times are simulated.
32 devices in a mesh: seq: 4 (over y, core), chan: 8 (over z, x).
Axes of the slice: x: 2, y: 2, z: 4, core: 2. Of those that a mesh axis runs over, the one named last changes fastest.
Arguments:
- query_rows: bfloat16 [512, 8192], P('seq', 'chan'), may hold values from -6 to 6
- key_rows: bfloat16 [512, 8192], P('seq', 'chan'), may hold values from -6 to 6
- value_rows: bfloat16 [512, 8192], P('seq', 'chan'), may hold values from -6 to 6
- short_taps: float32 [3, 3, 8192], P(None, None, 'chan'), may hold values from -3.5 to 3.5
- long_filter: float32 [512, 128], P('seq'), may hold values from -1.1 to 1.1
- cotangent: bfloat16 [512, 8192], P('seq', 'chan'), may hold values from -6 to 6
Outputs:
- hyena_out: bfloat16 [512, 8192], P('seq', 'chan')
- grad_query: bfloat16 [512, 8192], P('seq', 'chan')
- grad_key: bfloat16 [512, 8192], P('seq', 'chan')
- grad_value: bfloat16 [512, 8192], P('seq', 'chan')
- grad_filter: float32 [512, 128], P('seq')
All inputs are finite; a program needn't handle non-finite values.
Results may differ from a plain program's by a relative error of at most 0.001.
Values may be sent and summed in bfloat16 or wider, within the bound.
No kernel may reach another device: no remote copies, remote signals or barrier semaphores. Data moves between devices by JAX's collectives and lax.ppermute only.
A program may use at most 64 MiB of HBM per device.

v0:
```python
import math

import jax
import jax.numpy as jnp
import numpy as np
from jax import lax
from jax.sharding import PartitionSpec as P


def shifted(block, axis, distance):
    devices = range(lax.axis_size(axis))
    route = [(i - distance, i) for i in devices if i - distance in devices]
    return lax.ppermute(block, axis, route)


def product(matrix, operand, pattern):
    return jnp.einsum(pattern, matrix, operand, precision=lax.Precision.HIGHEST)


def phase_table(outer_size, inner_size, period, offset):
    column = lax.iota(jnp.int32, outer_size)[:, None]
    row_index = offset + lax.iota(jnp.int32, inner_size)[None, :]
    turn_count = column * row_index % period
    phase_angle = turn_count.astype(jnp.float32) * (2.0 * math.pi / period)
    return (jnp.cos(phase_angle), jnp.sin(phase_angle))


def forward_first(values, offset, period):
    blocks = values.shape[0]
    slab_rows = values.shape[1]
    cosine_table, sine_table = phase_table(2 * blocks, blocks, 2 * blocks, 0)
    real_part = product(cosine_table, values, "kn,njw->kjw")
    imag_part = -product(sine_table, values, "kn,njw->kjw")
    twist_cos, twist_sin = phase_table(2 * blocks, slab_rows, period, offset)
    twist_cos = twist_cos[:, :, None]
    twist_sin = twist_sin[:, :, None]
    return jnp.stack(
        [
            real_part * twist_cos + imag_part * twist_sin,
            imag_part * twist_cos - real_part * twist_sin,
        ],
        axis=2,
    )


def forward_second(mixed_in):
    length = mixed_in.shape[1]
    cosine_table, sine_table = phase_table(length, length, length, 0)
    real_in = mixed_in[:, :, 0]
    imag_in = mixed_in[:, :, 1]
    pattern = "mn,anw->amw"
    real_out = product(cosine_table, real_in, pattern) + product(sine_table, imag_in, pattern)
    imag_out = product(cosine_table, imag_in, pattern) - product(sine_table, real_in, pattern)
    return (real_out, imag_out)


def inverse_first(real_in, imag_in, groups):
    length = real_in.shape[1]
    cosine_table, sine_table = phase_table(length, length, length, 0)
    cosine_table = cosine_table.reshape(groups, length // groups, length)
    sine_table = sine_table.reshape(groups, length // groups, length)
    pattern = "gjm,amw->gajw"
    real_out = product(cosine_table, real_in, pattern) - product(sine_table, imag_in, pattern)
    imag_out = product(cosine_table, imag_in, pattern) + product(sine_table, real_in, pattern)
    return jnp.stack([real_out, imag_out], axis=3)


def inverse_second(spectral, offset, period, blocks):
    slab_rows = spectral.shape[1]
    twist_cos, twist_sin = phase_table(2 * blocks, slab_rows, period, offset)
    twist_cos = twist_cos[:, :, None]
    twist_sin = twist_sin[:, :, None]
    real_in = spectral[:, :, 0]
    imag_in = spectral[:, :, 1]
    real_turn = real_in * twist_cos - imag_in * twist_sin
    imag_turn = real_in * twist_sin + imag_in * twist_cos
    cosine_table, sine_table = phase_table(blocks, 2 * blocks, 2 * blocks, 0)
    pattern = "nk,kjw->njw"
    return (product(cosine_table, real_turn, pattern) - product(sine_table, imag_turn, pattern)) * (
        1.0 / period
    )


def to_channels(values):
    return lax.all_to_all(values, "seq", split_axis=1, concat_axis=0, tiled=True)


def to_blocks(values):
    return lax.all_to_all(values, "seq", split_axis=0, concat_axis=1, tiled=True)


def local_forward(signal):
    blocks = lax.axis_size("seq")
    total_len, channels = signal.shape
    length = total_len // blocks
    return forward_second(forward_first(signal.reshape(blocks, length, channels), 0, 2 * total_len))


def local_inverse(real_in, imag_in):
    blocks = lax.axis_size("seq")
    length = real_in.shape[1]
    channels = real_in.shape[2]
    spectral = inverse_first(real_in, imag_in, 1).reshape(2 * blocks, length, 2, channels)
    return inverse_second(spectral, 0, 2 * blocks * length, blocks).reshape(
        blocks * length, channels
    )


def complex_mul(left_re, left_im, right_re, right_im):
    return (left_re * right_re - left_im * right_im, left_re * right_im + left_im * right_re)


def conj_mul(left_re, left_im, right_re, right_im):
    return (left_re * right_re + left_im * right_im, left_re * right_im - left_im * right_re)


def group_sum(values, groups):
    return values.reshape(values.shape[:-1] + (values.shape[-1] // groups, groups)).sum(axis=-2)


def causal_taps(signal, previous, tap_weights):
    margin = previous.shape[0]
    length = signal.shape[0]
    extended = jnp.concatenate([previous.astype(jnp.float32), signal.astype(jnp.float32)], axis=0)
    summed = tap_weights[0] * extended[margin : margin + length]
    for shift_by in range(1, tap_weights.shape[0]):
        summed = (
            summed
            + tap_weights[shift_by] * extended[margin - shift_by : margin - shift_by + length]
        )
    return summed


def anticausal_taps(signal, following, tap_weights):
    length = signal.shape[0]
    extended = jnp.concatenate([signal, following], axis=0)
    summed = tap_weights[0] * signal
    for shift_by in range(1, tap_weights.shape[0]):
        summed = summed + tap_weights[shift_by] * extended[shift_by : shift_by + length]
    return summed


def per_device(query_rows, key_rows, value_rows, short_taps, long_filter, cotangent):
    length, channels = query_rows.shape
    groups = long_filter.shape[1]
    margin = short_taps.shape[1] - 1
    lead_query, lead_key, lead_value = shifted(
        (query_rows[length - margin :], key_rows[length - margin :], value_rows[length - margin :]),
        "seq",
        1,
    )
    query_conv = causal_taps(query_rows, lead_query, short_taps[0])
    key_conv = causal_taps(key_rows, lead_key, short_taps[1])
    value_conv = causal_taps(value_rows, lead_value, short_taps[2])
    gated_rows = key_conv * value_conv
    incoming = cotangent.astype(jnp.float32)
    conv_grad = incoming * query_conv
    blocks = lax.axis_size("seq")
    slice_width = channels // blocks
    distinct = min(slice_width, groups)
    picked = (
        (np.arange(blocks)[:, None] * slice_width + np.arange(distinct)[None, :]) % groups
    ).reshape(-1)
    filter_send = long_filter[:, picked]
    gated_part, filter_part = to_channels((gated_rows, filter_send))
    spec_re, spec_im = local_forward(jnp.concatenate([gated_part, filter_part], axis=1))
    gated_re, gated_im = (spec_re[:, :, :slice_width], spec_im[:, :, :slice_width])
    repeat = slice_width // distinct
    filter_re = jnp.tile(spec_re[:, :, slice_width:], (1, 1, repeat))
    filter_im = jnp.tile(spec_im[:, :, slice_width:], (1, 1, repeat))
    long_conv = to_blocks(local_inverse(*complex_mul(gated_re, gated_im, filter_re, filter_im)))
    grad_re, grad_im = local_forward(to_channels(conv_grad))
    back_re, back_im = conj_mul(filter_re, filter_im, grad_re, grad_im)
    cross_re, cross_im = conj_mul(gated_re, gated_im, grad_re, grad_im)
    combined = local_inverse(
        jnp.concatenate([back_re, cross_re], axis=2), jnp.concatenate([back_im, cross_im], axis=2)
    )
    gated_grad, filter_rows = to_blocks((combined[:, :slice_width], combined[:, slice_width:]))
    filter_local = group_sum(filter_rows, groups)
    hyena_out = (query_conv * long_conv).astype(jnp.bfloat16)
    query_grad = incoming * long_conv
    grad_filter = lax.psum(filter_local, "chan")
    key_grad = gated_grad * value_conv
    value_grad = gated_grad * key_conv
    next_query, next_key, next_value = shifted(
        (query_grad[:margin], key_grad[:margin], value_grad[:margin]), "seq", -1
    )
    grad_query = anticausal_taps(query_grad, next_query, short_taps[0]).astype(jnp.bfloat16)
    grad_key = anticausal_taps(key_grad, next_key, short_taps[1]).astype(jnp.bfloat16)
    grad_value = anticausal_taps(value_grad, next_value, short_taps[2]).astype(jnp.bfloat16)
    return (hyena_out, grad_query, grad_key, grad_value, grad_filter)


def solution(mesh):
    in_specs = (
        P("seq", "chan"),
        P("seq", "chan"),
        P("seq", "chan"),
        P(None, None, "chan"),
        P("seq", None),
        P("seq", "chan"),
    )
    out_specs = (
        P("seq", "chan"),
        P("seq", "chan"),
        P("seq", "chan"),
        P("seq", "chan"),
        P("seq", None),
    )
    return jax.shard_map(
        per_device, mesh=mesh, in_specs=in_specs, out_specs=out_specs, check_vma=False
    )
```

profile of v0, /device:TPU:0, one launch (start us, length us, event | category | flops | bytes accessed | tf_op | source)
XLA Modules:
  0.0 229.1 jit_solution(14020881731638315030)
XLA Ops:
  10.8 4.2 %all-to-all-start.1 = ((f32[128,4,128]{2,0,1:T(8,128)}), f32[128,4,128]{2,0,1:T(8,128)S(1)}, u32[]{:S(2)}, u32[]{:S(2)}) async-start(f32[128,4,128]{2,0,1:T(8,128)} %copy.156), calls=%async_computation.1 | async-start | bytes 524288 | tf_op jit(solution)/shard_map/all_to_all | solution.py:85
  15.2 2.4 %collective-permute-start = (bf16[2,1024]{0,1:T(8,128)(2,1)S(1)}, bf16[2,1024]{0,1:T(8,128)(2,1)S(1)}, u32[]{:S(2)}, u32[]{:S(2)}) collective-permute-start(bf16[2,1024]{0,1:T(8,128)(2,1)S(1)} %copy.148), channel_id=1, source_target_pairs={{0,8},{8,16},{16,24},{1,9},{9,17},{17,25},{2,10},{10,18},{18,26},{... | collective-permute-start | bytes 12296 | tf_op jit(solution)/shard_map/ppermute | solution.py:13
  17.9 3.7 %collective-permute-start.1 = (bf16[2,1024]{0,1:T(8,128)(2,1)S(1)}, bf16[2,1024]{0,1:T(8,128)(2,1)S(1)}, u32[]{:S(2)}, u32[]{:S(2)}) collective-permute-start(bf16[2,1024]{0,1:T(8,128)(2,1)S(1)} %copy.150), channel_id=1, source_target_pairs={{0,8},{8,16},{16,24},{1,9},{9,17},{17,25},{2,10},{10,18},{18,26},{... | collective-permute-start | bytes 12296 | tf_op jit(solution)/shard_map/ppermute | solution.py:13
  27.6 3.5 %all-to-all-start.3 = ((f32[128,4,256]{2,0,1:T(8,128)}), f32[128,4,256]{2,0,1:T(8,128)S(1)}, u32[]{:S(2)}, u32[]{:S(2)}) async-start(f32[128,4,256]{2,0,1:T(8,128)} %copy.169), calls=%async_computation.3 | async-start | bytes 1048576 | tf_op jit(solution)/shard_map/all_to_all | solution.py:85
  31.9 3.5 %fusion.240 = (f32[128,1024]{0,1:T(8,128)S(1)}, f32[128,1024]{0,1:T(8,128)}, f32[128,1024]{0,1:T(8,128)}) fusion(f32[128,1024]{0,1:T(8,128)S(1)} %convert_element_type.148, f32[2,1024]{0,1:T(8,128)S(1)} %convert_element_type.149, f32[1024]{0:T(1024)S(1)} %bitcast.217, f32[1024]{0:T(1024)} %bitcast.219, f32[1024]{0:T(1024)S(1)} %bitcast.215, ...), kind=kLoop, calls=%fused_computation.292 | loop fusion | flops 1966080 | bytes 2662400 | tf_op jit(solution)/shard_map/mul | solution.py:155
  37.6 2.3 %all-to-all-done.3 = f32[128,4,256]{2,0,1:T(8,128)S(1)} async-done(((f32[128,4,256]{2,0,1:T(8,128)}), f32[128,4,256]{2,0,1:T(8,128)S(1)}, u32[]{:S(2)}, u32[]{:S(2)}) %all-to-all-start.3) | async-done | bytes 524320 | tf_op jit(solution)/shard_map/all_to_all | solution.py:85
  39.9 4.7 %all-to-all-start = ((f32[128,4,256]{2,0,1:T(8,128)}), f32[128,4,256]{2,0,1:T(8,128)}, u32[]{:S(2)}, u32[]{:S(2)}) async-start(f32[128,4,256]{2,0,1:T(8,128)} %copy.153), calls=%async_computation | async-start | bytes 1048576 | tf_op jit(solution)/shard_map/all_to_all | solution.py:85
  46.5 2.5 %fusion.49 = f32[8,128,256]{2,0,1:T(8,128)} fusion(f32[128,4,256]{2,0,1:T(8,128)S(1)} %all-to-all-done.3), kind=kOutput, calls=%fused_computation.110 | convolution fusion | flops 12583360 | bytes 1572864 | tf_op jit(solution)/shard_map/kn,njw->kjw/dot_general | solution.py:17
  59.6 4.4 %multiply_add_fusion.1 = (f32[8,128,384]{2,0,1:T(8,128)}, f32[8,128,384]{2,0,1:T(8,128)}) fusion(f32[8,128,384]{2,0,1:T(8,128)S(1)} %fusion.52, f32[8,128]{0,1:T(8,128)S(1)} %copy.159, f32[8,128]{0,1:T(8,128)S(1)} %copy.158, f32[4,128,128]{2,0,1:T(4,128)S(1)} %bitcast.205, f32[4,128,256]{2,0,1:T(4,128)S(1)} %bitcast.202), kind=kOutput, calls=%fused_computation.26 | convolution fusion | flops 21823936 | bytes 5513216 | tf_op jit(solution)/shard_map/kn,njw->kjw/dot_general | solution.py:17
  64.0 3.0 %copy.160 = f32[8,128,384]{1,2,0:T(8,128)} copy(f32[8,128,384]{2,0,1:T(8,128)} %get-tuple-element.36) | data formatting | bytes 3145728 | tf_op jit(solution)/shard_map/add | solution.py:39
  67.0 3.0 %copy.161 = f32[8,128,384]{1,2,0:T(8,128)} copy(f32[8,128,384]{2,0,1:T(8,128)} %get-tuple-element.37) | data formatting | bytes 3145728 | tf_op jit(solution)/shard_map/sub | solution.py:40
  70.1 3.2 %fusion.76 = f32[8,384,128]{2,1,0:T(8,128)S(1)} fusion(f32[8,128,384]{1,2,0:T(8,128)} %copy.161), kind=kOutput, calls=%fused_computation.143 | convolution fusion | flops 604209152 | bytes 3145728 | tf_op jit(solution)/shard_map/mn,anw->amw/dot_general | solution.py:17
  80.0 2.9 %multiply_add_fusion.2 = (f32[8,128,256]{1,2,0:T(8,128)S(1)}, f32[8,128,256]{1,2,0:T(8,128)S(1)}, f32[8,128,256]{1,2,0:T(8,128)S(1)}, f32[8,128,256]{1,2,0:T(8,1...) fusion(f32[8,128,256]{1,2,0:T(8,128)S(1)} %copy-done.6, f32[8,128,384]{1,2,0:T(8,128)S(1)} %subtract_bitcast_fusion.1, ...), kind=kOutput, calls=%fused_computation.59 | convolution fusion | flops 408911872 | bytes 13639680 | tf_op jit(solution)/shard_map/mn,anw->amw/dot_general | solution.py:17
  82.9 3.6 %fusion = f32[8,512,128]{2,1,0:T(8,128)} fusion(f32[8,128,256]{1,2,0:T(8,128)S(1)} %get-tuple-element.31, f32[8,128,256]{1,2,0:T(8,128)S(1)} %get-tuple-element.42), kind=kOutput, calls=%fused_computation.19 | convolution fusion | flops 806060032 | bytes 4194304 | tf_op jit(solution)/shard_map/gjm,amw->gajw/dot_general | solution.py:17
  86.5 3.4 %fusion.1 = f32[8,512,128]{2,1,0:T(8,128)} fusion(f32[8,128,256]{1,2,0:T(8,128)S(1)} %get-tuple-element.31, f32[8,128,256]{1,2,0:T(8,128)S(1)} %get-tuple-element.42), kind=kOutput, calls=%fused_computation.20 | convolution fusion | flops 806060032 | bytes 4194304 | tf_op jit(solution)/shard_map/gjm,amw->gajw/dot_general | solution.py:17
  101.5 3.9 %all-to-all-start.2 = ((f32[4,128,256]{2,1,0:T(8,128)}), f32[4,128,256]{2,1,0:T(8,128)S(1)}, u32[]{:S(2)}, u32[]{:S(2)}) async-start(f32[4,128,256]{2,1,0:T(8,128)} %copy.166), calls=%async_computation.2 | async-start | bytes 1048576 | tf_op jit(solution)/shard_map/all_to_all | solution.py:89
  105.4 3.8 %subtract_bitcast_fusion = f32[1,8,128,1,512]{2,4,1,3,0:T(8,128)S(1)} fusion(f32[8,512,128]{2,1,0:T(8,128)} %fusion.1, f32[8,128,256]{1,2,0:T(8,128)S(1)} %get-tuple-element.30, f32[8,128,256]{1,2,0:T(8,128)S(1)} %copy-done.2), kind=kOutput, calls=%fused_computation.18 | convolution fusion | flops 806584320 | bytes 6291456 | tf_op jit(solution)/shard_map/gjm,amw->gajw/dot_general | solution.py:17
  113.6 3.1 %copy.175 = f32[8,128,512]{2,0,1:T(8,128)} copy(f32[8,128,512]{1,2,0:T(8,128)} %get-tuple-element.32) | data formatting | bytes 4194304 | tf_op jit(solution)/shard_map/add | solution.py:76
  118.7 3.6 %fusion.119 = f32[4,128,512]{2,0,1:T(4,128)S(1)} fusion(f32[8,128,512]{2,0,1:T(8,128)} %copy.174), kind=kOutput, calls=%fused_computation.180 | convolution fusion | flops 25166272 | bytes 3145728 | tf_op jit(solution)/shard_map/nk,kjw->njw/dot_general | solution.py:17
  125.6 3.5 %all-to-all-start.4 = ((f32[4,128,256]{2,1,0:T(8,128)}), f32[4,128,256]{2,1,0:T(8,128)S(1)}, u32[]{:S(2)}, u32[]{:S(2)}) async-start(f32[4,128,256]{2,1,0:T(8,128)} %bitcast.50), calls=%async_computation.4 | async-start | bytes 1048576 | tf_op jit(solution)/shard_map/all_to_all | solution.py:89
  130.1 7.8 %all-to-all-done.4 = f32[4,128,256]{2,1,0:T(8,128)S(1)} async-done(((f32[4,128,256]{2,1,0:T(8,128)}), f32[4,128,256]{2,1,0:T(8,128)S(1)}, u32[]{:S(2)}, u32[]{:S(2)}) %all-to-all-start.4) | async-done | bytes 524320 | tf_op jit(solution)/shard_map/all_to_all | solution.py:89
  137.9 3.5 %all-to-all-start.5 = ((f32[4,128,256]{1,2,0:T(8,128)}), f32[4,128,256]{1,2,0:T(8,128)S(1)}, u32[]{:S(2)}, u32[]{:S(2)}) async-start(f32[4,128,256]{1,2,0:T(8,128)} %copy.178), calls=%async_computation.5 | async-start | bytes 1048576 | tf_op jit(solution)/shard_map/all_to_all | solution.py:89
  146.9 3.3 %all-to-all-done.5 = f32[4,128,256]{1,2,0:T(8,128)S(1)} async-done(((f32[4,128,256]{1,2,0:T(8,128)}), f32[4,128,256]{1,2,0:T(8,128)S(1)}, u32[]{:S(2)}, u32[]{:S(2)}) %all-to-all-start.5) | async-done | bytes 524320 | tf_op jit(solution)/shard_map/all_to_all | solution.py:89
  160.7 59.8 %all-reduce.2.cloned.1.call-done = f32[128,128]{0,1:T(8,128)} async-done(((f32[128,128]{0,1:T(8,128)}), f32[128,128]{0,1:T(8,128)}) %all-reduce.2.cloned.1.call-update) | async-done | bytes 65552 | tf_op jit(solution)/shard_map/psum | solution.py:182
  (138 shorter events, 71.6 us)
Async XLA Ops:
  7.2 7.9 %copy-start.10 = (bf16[128,1024]{1,0:T(8,128)(2,1)S(1)}, bf16[128,1024]{1,0:T(8,128)(2,1)}, u32[]{:S(2)}) copy-start(bf16[128,1024]{1,0:T(8,128)(2,1)} %param.8) | copy-start | bytes 786436
  7.2 10.5 %copy-start.11 = (bf16[128,1024]{1,0:T(8,128)(2,1)S(1)}, bf16[128,1024]{1,0:T(8,128)(2,1)}, u32[]{:S(2)}) copy-start(bf16[128,1024]{1,0:T(8,128)(2,1)} %param.9) | copy-start | bytes 786436
  7.2 14.4 %copy-start.12 = (bf16[128,1024]{1,0:T(8,128)(2,1)S(1)}, bf16[128,1024]{1,0:T(8,128)(2,1)}, u32[]{:S(2)}) copy-start(bf16[128,1024]{1,0:T(8,128)(2,1)} %param.10) | copy-start | bytes 786436
  8.9 14.9 %copy-start.24 = (f32[3,3,1024]{2,1,0:T(4,128)S(1)}, f32[3,3,1024]{2,1,0:T(4,128)}, u32[]{:S(2)}) copy-start(f32[3,3,1024]{2,1,0:T(4,128)} %param.11) | copy-start | bytes 110596
  8.9 15.7 %copy-start.13 = (bf16[128,1024]{1,0:T(8,128)(2,1)S(1)}, bf16[128,1024]{1,0:T(8,128)(2,1)}, u32[]{:S(2)}) copy-start(bf16[128,1024]{1,0:T(8,128)(2,1)} %param.13) | copy-start | bytes 786436
  10.8 16.8 %all-to-all-start.1 = ((f32[128,4,128]{2,0,1:T(8,128)}), f32[128,4,128]{2,0,1:T(8,128)S(1)}, u32[]{:S(2)}, u32[]{:S(2)}) async-start(f32[128,4,128]{2,0,1:T(8,128)} %copy.156), calls=%async_computation.1 | async-start | bytes 524288 | tf_op jit(solution)/shard_map/all_to_all | solution.py:85
  15.2 9.6 %collective-permute-start = (bf16[2,1024]{0,1:T(8,128)(2,1)S(1)}, bf16[2,1024]{0,1:T(8,128)(2,1)S(1)}, u32[]{:S(2)}, u32[]{:S(2)}) collective-permute-start(bf16[2,1024]{0,1:T(8,128)(2,1)S(1)} %copy.148), channel_id=1, source_target_pairs={{0,8},{8,16},{16,24},{1,9},{9,17},{17,25},{2,10},{10,18},{18,26},{... | collective-permute-start | bytes 12296 | tf_op jit(solution)/shard_map/ppermute | solution.py:13
  17.9 13.9 %collective-permute-start.1 = (bf16[2,1024]{0,1:T(8,128)(2,1)S(1)}, bf16[2,1024]{0,1:T(8,128)(2,1)S(1)}, u32[]{:S(2)}, u32[]{:S(2)}) collective-permute-start(bf16[2,1024]{0,1:T(8,128)(2,1)S(1)} %copy.150), channel_id=1, source_target_pairs={{0,8},{8,16},{16,24},{1,9},{9,17},{17,25},{2,10},{10,18},{18,26},{... | collective-permute-start | bytes 12296 | tf_op jit(solution)/shard_map/ppermute | solution.py:13
  21.8 10.0 %collective-permute-start.2 = (bf16[2,1024]{0,1:T(8,128)(2,1)S(1)}, bf16[2,1024]{0,1:T(8,128)(2,1)S(1)}, u32[]{:S(2)}, u32[]{:S(2)}) collective-permute-start(bf16[2,1024]{0,1:T(8,128)(2,1)S(1)} %copy.152), channel_id=1, source_target_pairs={{0,8},{8,16},{16,24},{1,9},{9,17},{17,25},{2,10},{10,18},{18,26},{... | collective-permute-start | bytes 12296 | tf_op jit(solution)/shard_map/ppermute | solution.py:13
  27.6 12.3 %all-to-all-start.3 = ((f32[128,4,256]{2,0,1:T(8,128)}), f32[128,4,256]{2,0,1:T(8,128)S(1)}, u32[]{:S(2)}, u32[]{:S(2)}) async-start(f32[128,4,256]{2,0,1:T(8,128)} %copy.169), calls=%async_computation.3 | async-start | bytes 1048576 | tf_op jit(solution)/shard_map/all_to_all | solution.py:85
  39.9 16.5 %all-to-all-start = ((f32[128,4,256]{2,0,1:T(8,128)}), f32[128,4,256]{2,0,1:T(8,128)}, u32[]{:S(2)}, u32[]{:S(2)}) async-start(f32[128,4,256]{2,0,1:T(8,128)} %copy.153), calls=%async_computation | async-start | bytes 1048576 | tf_op jit(solution)/shard_map/all_to_all | solution.py:85
  101.5 24.1 %all-to-all-start.2 = ((f32[4,128,256]{2,1,0:T(8,128)}), f32[4,128,256]{2,1,0:T(8,128)S(1)}, u32[]{:S(2)}, u32[]{:S(2)}) async-start(f32[4,128,256]{2,1,0:T(8,128)} %copy.166), calls=%async_computation.2 | async-start | bytes 1048576 | tf_op jit(solution)/shard_map/all_to_all | solution.py:89
  125.6 12.3 %all-to-all-start.4 = ((f32[4,128,256]{2,1,0:T(8,128)}), f32[4,128,256]{2,1,0:T(8,128)S(1)}, u32[]{:S(2)}, u32[]{:S(2)}) async-start(f32[4,128,256]{2,1,0:T(8,128)} %bitcast.50), calls=%async_computation.4 | async-start | bytes 1048576 | tf_op jit(solution)/shard_map/all_to_all | solution.py:89
  137.9 12.3 %all-to-all-start.5 = ((f32[4,128,256]{1,2,0:T(8,128)}), f32[4,128,256]{1,2,0:T(8,128)S(1)}, u32[]{:S(2)}, u32[]{:S(2)}) async-start(f32[4,128,256]{1,2,0:T(8,128)} %copy.178), calls=%async_computation.5 | async-start | bytes 1048576 | tf_op jit(solution)/shard_map/all_to_all | solution.py:89
  141.4 79.1 %all-reduce.2.cloned.1.call-start = ((), (), s32[]{:S(2)}) async-start(), calls=%async_computation.6 | async-start | bytes 131072 | tf_op jit(solution)/shard_map/psum | solution.py:182
  141.7 9.3 %copy-start.7 = (f32[128,1024]{0,1:T(8,128)S(1)}, f32[128,1024]{0,1:T(8,128)}, u32[]{:S(2)}) copy-start(f32[128,1024]{0,1:T(8,128)} %get-tuple-element.28) | copy-start | bytes 1572868
  141.7 9.3 %copy-start.8 = (f32[128,1024]{0,1:T(8,128)S(1)}, f32[128,1024]{0,1:T(8,128)}, u32[]{:S(2)}) copy-start(f32[128,1024]{0,1:T(8,128)} %get-tuple-element.29) | copy-start | bytes 1572868
  145.4 8.4 %collective-permute-start.3 = (f32[2,1024]{0,1:T(8,128)S(1)}, f32[2,1024]{0,1:T(8,128)}, u32[]{:S(2)}, u32[]{:S(2)}) collective-permute-start(f32[2,1024]{0,1:T(8,128)S(1)} %bitcast.211), channel_id=1, source_target_pairs={{8,0},{16,8},{24,16},{9,1},{17,9},{25,17},{10,2},{18,10},{26,18},{... | collective-permute-start | bytes 24584 | tf_op jit(solution)/shard_map/ppermute | solution.py:13
  146.7 7.1 %copy-start.19 = (f32[1,1,1024]{2,1,0:T(1,128)S(1)}, f32[1,1,1024]{2,1,0:T(1,128)}, u32[]{:S(2)}) copy-start(f32[1,1,1024]{2,1,0:T(1,128)} %copy-done.18) | copy-start | bytes 12292
  146.7 7.1 %copy-start.21 = (f32[1,1,1024]{2,1,0:T(1,128)S(1)}, f32[1,1,1024]{2,1,0:T(1,128)}, u32[]{:S(2)}) copy-start(f32[1,1,1024]{2,1,0:T(1,128)} %copy-done.20) | copy-start | bytes 12292
  146.7 7.1 %copy-start.23 = (f32[1,1,1024]{2,1,0:T(1,128)S(1)}, f32[1,1,1024]{2,1,0:T(1,128)}, u32[]{:S(2)}) copy-start(f32[1,1,1024]{2,1,0:T(1,128)} %copy-done.22) | copy-start | bytes 12292
  150.9 6.2 %copy-start.14 = (f32[1,1,1024]{2,1,0:T(1,128)S(1)}, f32[1,1,1024]{2,1,0:T(1,128)}, u32[]{:S(2)}) copy-start(f32[1,1,1024]{2,1,0:T(1,128)} %get-tuple-element.60) | copy-start | bytes 12292
  151.0 5.0 %collective-permute-start.4 = (f32[2,1024]{0,1:T(8,128)S(1)}, f32[2,1024]{0,1:T(8,128)S(1)}, u32[]{:S(2)}, u32[]{:S(2)}) collective-permute-start(f32[2,1024]{0,1:T(8,128)S(1)} %bitcast.207), channel_id=1, source_target_pairs={{8,0},{16,8},{24,16},{9,1},{17,9},{25,17},{10,2},{18,10},{26,18},{... | collective-permute-start | bytes 24584 | tf_op jit(solution)/shard_map/ppermute | solution.py:13
  152.3 4.8 %collective-permute-start.5 = (f32[2,1024]{0,1:T(8,128)S(1)}, f32[2,1024]{0,1:T(8,128)S(1)}, u32[]{:S(2)}, u32[]{:S(2)}) collective-permute-start(f32[2,1024]{0,1:T(8,128)S(1)} %bitcast.206), channel_id=1, source_target_pairs={{8,0},{16,8},{24,16},{9,1},{17,9},{25,17},{10,2},{18,10},{26,18},{... | collective-permute-start | bytes 24584 | tf_op jit(solution)/shard_map/ppermute | solution.py:13
  (14 other events, 47.2 us)
Sparse Core Ops, SparseCore 0:
  151.0 69.3 all-reduce.1
where the time goes:
time: 234 us; the launch traced here: 229 us
  waiting for transfers between devices  73.2 us (31%)
  matrix products  52.8 us (23%)
  local copies, waits for them, and re-layouts  35.8 us (15%)
  starting transfers between devices  35.3 us (15%)
  other arithmetic  17 us (7%)
  between operations  15 us (6%)
    psum x1, waiting for transfers between devices, per_device(): grad_filter = lax.psum(filter_local, 'chan')  59.8 us
    dot_general x24, matrix products, product(): return jnp.einsum(pattern, matrix, operand, precision=lax.Precision.HIGHEST)  52.8 us
    all_to_all x3, starting transfers between devices, to_channels(): lax.all_to_all(values, 'seq', split_axis=1, concat_axis=0, tiled=True)  12.4 us
    ppermute x6, starting transfers between devices, shifted(): return lax.ppermute(block, axis, route)  12.1 us
    all_to_all x3, waiting for transfers between devices, to_blocks(): lax.all_to_all(values, 'seq', split_axis=0, concat_axis=1, tiled=True)  11.1 us
    all_to_all x3, starting transfers between devices, to_blocks(): lax.all_to_all(values, 'seq', split_axis=0, concat_axis=1, tiled=True)  10.8 us
    unnamed x60, local copies, waits for them, and re-layouts  9.05 us
    all_to_all x5, local copies, waits for them, and re-layouts, to_channels(): lax.all_to_all(values, 'seq', split_axis=1, concat_axis=0, tiled=True)  5.37 us
  transfers between devices with their start and end apart: 13, of which 4 were waited for; matrix products, arithmetic and copies ran while one was open for 24% of the time, Pallas kernels for 0%

commit v1 on v0

v1 whole, which is shorter than its diff:
```python
import functools

import jax
import jax.numpy as jnp
import ml_dtypes
import numpy as np
from jax import lax
from jax.experimental import pallas as pl
from jax.experimental.pallas import tpu as pltpu
from jax.sharding import PartitionSpec as P

F32 = jnp.float32
BF16 = jnp.bfloat16
EDGE = 8
HALO = 16
VMEM = pl.BlockSpec(memory_space=pltpu.VMEM)


def split_table(table):
    high = table.astype(ml_dtypes.bfloat16)
    low = (table - high.astype(np.float64)).astype(ml_dtypes.bfloat16)
    return high, low


def dft_tables(length):
    frequency = np.pi * (2 * np.arange(length) + 1) / (2 * length)
    into = frequency[:, None] * np.arange(length)[None, :]
    high, low = split_table(np.concatenate([np.cos(into), -np.sin(into)], axis=0))
    forward = np.concatenate([high, high, low], axis=1)
    back = np.arange(length + EDGE)[:, None] * frequency[None, :]
    high, low = split_table(np.concatenate([np.cos(back), -np.sin(back)], axis=1) / length)
    inverse = np.concatenate([high, high, low], axis=1)
    return jnp.asarray(forward), jnp.asarray(inverse)


def halves(values):
    high = values.astype(BF16)
    return high, (values - high.astype(F32)).astype(BF16)


def table_dot(table, values):
    high, low = halves(values)
    return jnp.dot(
        table, jnp.concatenate([high, low, high], axis=0), preferred_element_type=F32
    )


def pack_kernel(bits, q_ref, k_ref, v_ref, c_ref, filter_ref, *unit_refs):
    length, width = q_ref.shape
    groups = filter_ref.shape[1]
    rows = length * groups // width
    me = lax.axis_index("seq")
    filter_high, filter_low = halves(filter_ref[...])
    for bit, unit in zip(bits, unit_refs):
        first = 2 * length
        for tile in range(width // groups):
            lanes = slice(tile * groups, (tile + 1) * groups)
            unit[first : first + rows, lanes] = filter_high[tile * rows : (tile + 1) * rows]
            unit[first + rows : first + 2 * rows, lanes] = filter_low[
                tile * rows : (tile + 1) * rows
            ]
        first += 2 * rows
        low_side = (me // bit) % 2 == 0

        @pl.when(low_side)
        def _():
            unit[0:length] = k_ref[...]
            unit[length : 2 * length] = v_ref[...]
            unit[first : first + HALO] = q_ref[length - HALO : length]

        @pl.when(jnp.logical_not(low_side))
        def _():
            unit[0:length] = q_ref[...]
            unit[length : 2 * length] = c_ref[...]
            unit[first : first + HALO] = jnp.concatenate(
                [k_ref[0:HALO].astype(F32)[0:EDGE], v_ref[0:HALO].astype(F32)[0:EDGE]], axis=0
            ).astype(BF16)


def taps_of(rows_ref, slot, count, weights, lanes_out=None):
    total = weights[0:1] * rows_ref[slot, EDGE : EDGE + count]
    for shift in range(1, weights.shape[0]):
        total = total + weights[shift : shift + 1] * rows_ref[
            slot, EDGE - shift : EDGE - shift + count
        ]
    return total


def main_kernel(
    blocks,
    tile_width,
    q_ref,
    k_ref,
    v_ref,
    c_ref,
    taps_ref,
    filter_ref,
    forward_ref,
    inverse_ref,
    *refs,
):
    units = refs[: blocks - 1]
    out_ref, gq_ref, gk_ref, gv_ref, gf_ref = refs[blocks - 1 : blocks + 4]
    first_rows, second_rows, spectra, filter_rows, cross, own_spec, acc, fix, grads = refs[
        blocks + 4 :
    ]
    length, width = q_ref.shape
    groups = filter_ref.shape[1]
    rows = length * groups // width
    me = lax.axis_index("seq")
    forward = forward_ref[...]
    sign = jnp.where(lax.broadcasted_iota(jnp.int32, (length, groups), 0) % 2 == 0, 1.0, -1.0)

    for edge in (0, 1, blocks + 2):
        filter_rows[edge] = jnp.zeros((length, groups), F32)
    filter_rows[me + 2] = filter_ref[...]
    for index, unit in enumerate(units):
        pieces = []
        for tile in range(width // groups):
            lanes = slice(tile * groups, (tile + 1) * groups)
            pieces.append(
                unit[2 * length : 2 * length + rows, lanes].astype(F32)
                + unit[2 * length + rows : 2 * length + 2 * rows, lanes].astype(F32)
            )
        filter_rows[(me ^ (index + 1)) + 2] = jnp.concatenate(pieces, axis=0)
    previous = None
    for distance in range(blocks):
        own = table_dot(forward, filter_rows[distance + 2])
        if previous is None:
            spectra[distance] = own
        else:
            spectra[distance, 0:length] = own[0:length] - sign * previous[length:]
            spectra[distance, length:] = own[length:] + sign * previous[0:length]
        previous = own
    cross[...] = jnp.zeros(cross.shape, F32)

    def wide(values):
        return jnp.concatenate([values] * (tile_width // groups), axis=1)

    def filter_row(block, row):
        return wide(filter_rows[block + 2, pl.ds(row, 1)])

    def one_tile(step, carry):
        lanes = pl.ds(pl.multiple_of(step * tile_width, tile_width), tile_width)
        weights = [taps_ref[p, :, lanes] for p in range(3)]
        zero_edge = jnp.zeros((EDGE, tile_width), F32)

        first_rows[0, 0:EDGE] = zero_edge
        second_rows[0, 0:EDGE] = zero_edge
        first_rows[me + 1, 0:EDGE] = zero_edge

        @pl.when(me == blocks - 1)
        def _():
            for slot in (me, me + 1):
                first_rows[slot, EDGE + length :] = zero_edge
                second_rows[slot, EDGE + length :] = zero_edge

        def place(slot, one, two):
            first_rows[slot, EDGE : EDGE + length] = one
            second_rows[slot, EDGE : EDGE + length] = two

        def own_pair(slot, one, two):
            place(slot, one[:, lanes].astype(F32), two[:, lanes].astype(F32))

        own_pair(me, k_ref, v_ref)
        own_pair(me + 1, q_ref, c_ref)

        first_rows[me + 2, 0:EDGE] = first_rows[me + 1, length : length + EDGE]
        for index, unit in enumerate(units):
            other = me ^ (index + 1)
            lower = other < me
            slot = jnp.where(lower, other, other + 1)
            one = unit[0:length, lanes].astype(F32)
            two = unit[length : 2 * length, lanes].astype(F32)
            place(slot, one, two)
            first_rows[slot + 1, 0:EDGE] = one[length - EDGE :]
            second_rows[slot + 1, 0:EDGE] = two[length - EDGE :]
            edge = unit[2 * length + 2 * rows :, lanes].astype(F32)

            @pl.when(other == me + 1)
            def _():
                first_rows[me, EDGE + length :] = edge[0:EDGE]
                second_rows[me, EDGE + length :] = edge[EDGE:]
                first_rows[me + 1, EDGE + length :] = one[0:EDGE]
                second_rows[me + 1, EDGE + length :] = two[0:EDGE]

        for index, unit in enumerate(units):
            other = me ^ (index + 1)

            @pl.when(other == me - 1)
            def _():
                edge = unit[2 * length + 2 * rows :, lanes].astype(F32)
                first_rows[me + 1, 0:EDGE] = edge[EDGE:]

        fix[...] = jnp.zeros(fix.shape, F32)

        def filter_spec(distance):
            return (
                wide(spectra[distance, 0:length]),
                wide(spectra[distance, length:]),
            )

        def add_lower(distance, signal, spec, fresh):
            re, im = spec[0:length], spec[length:]
            h_re, h_im = filter_spec(distance)
            new_re = h_re * re - h_im * im
            new_im = h_re * im + h_im * re
            if fresh:
                acc[0, 0:length] = new_re
                acc[0, length:] = new_im
            else:
                acc[0, 0:length] += new_re
                acc[0, length:] += new_im
            c_re, c_im = own_spec[0:length], own_spec[length:]
            cross_re = re * c_re + im * c_im
            cross_im = re * c_im - im * c_re
            for tile in range(tile_width // groups):
                part = slice(tile * groups, (tile + 1) * groups)
                cross[distance, 0:length] += cross_re[:, part]
                cross[distance, length:] += cross_im[:, part]
            near = filter_row(distance + 1, 0) + filter_row(distance - 1, 0)
            far = filter_row(distance + 1, 1) + filter_row(distance - 1, 1)
            fix[0:1] += signal[0:1] * near
            fix[1:2] += signal[0:1] * far + signal[1:2] * near

        def add_upper(distance, signal, spec, fresh):
            re, im = spec[0:length], spec[length:]
            h_re, h_im = filter_spec(distance)
            new_re = h_re * re + h_im * im
            new_im = h_re * im - h_im * re
            if fresh:
                acc[1, 0:length] = new_re
                acc[1, length:] = new_im
            else:
                acc[1, 0:length] += new_re
                acc[1, length:] += new_im
            fix[EDGE + 1 : EDGE + 2] += signal[0:1] * (
                filter_row(distance - 2, length - 1) + filter_row(distance, length - 1)
            )

        count = length + EDGE
        query_conv = taps_of(first_rows, me + 1, count, weights[0])
        incoming = second_rows[me + 1, EDGE : EDGE + count]
        conv_grad = (query_conv * incoming)[0:length]
        own_spec[...] = table_dot(forward, conv_grad)
        add_upper(0, conv_grad, own_spec[...], True)
        key_conv = taps_of(first_rows, me, count, weights[1])
        value_conv = taps_of(second_rows, me, count, weights[2])
        gated = key_conv * value_conv
        add_lower(0, gated[0:length], table_dot(forward, gated[0:length]), True)
        after = gated[length : length + 2]
        zero_lag, one_lag = filter_row(0, 0), filter_row(0, 1)
        fix[0:1] += after[0:1] * zero_lag
        fix[1:2] += after[1:2] * zero_lag + after[0:1] * one_lag

        for index in range(blocks - 1):
            other = me ^ (index + 1)

            @pl.when(other < me)
            def _():
                signal = taps_of(first_rows, other, length, weights[1]) * taps_of(
                    second_rows, other, length, weights[2]
                )
                add_lower(me - other, signal, table_dot(forward, signal), False)

            @pl.when(other > me)
            def _():
                signal = (
                    taps_of(first_rows, other + 1, length, weights[0])
                    * second_rows[other + 1, EDGE : EDGE + length]
                )
                add_upper(other - me, signal, table_dot(forward, signal), False)

        inverse = inverse_ref[...]
        long_conv = table_dot(inverse, acc[0])
        gated_grad = table_dot(inverse, acc[1])
        out_ref[:, lanes] = (query_conv[0:length] * long_conv[0:length]).astype(BF16)
        inside = jnp.where(me < blocks - 1, 1.0, 0.0)
        conv_edge = long_conv[length:] + fix[0:EDGE]
        grad_edge = (gated_grad[length:] + fix[EDGE:]) * inside
        grads[0, 0:length] = incoming[0:length] * long_conv[0:length]
        grads[0, length:] = incoming[length:] * conv_edge
        grads[1, 0:length] = gated_grad[0:length] * value_conv[0:length]
        grads[1, length:] = grad_edge * value_conv[length:]
        grads[2, 0:length] = gated_grad[0:length] * key_conv[0:length]
        grads[2, length:] = grad_edge * key_conv[length:]
        for p, ref in enumerate((gq_ref, gk_ref, gv_ref)):
            total = weights[p][0:1] * grads[p, 0:length]
            for shift in range(1, weights[p].shape[0]):
                total = total + weights[p][shift : shift + 1] * grads[p, shift : shift + length]
            ref[:, lanes] = total.astype(BF16)
        return carry

    lax.fori_loop(0, width // tile_width, one_tile, 0)

    inverse = inverse_ref[0:length]
    for block in range(blocks):
        re, im = cross[block, 0:length], cross[block, length:]
        if block + 1 < blocks:
            re = re + sign * cross[block + 1, length:]
            im = im - sign * cross[block + 1, 0:length]
        gf_ref[block] = table_dot(inverse, jnp.concatenate([re, im], axis=0))


def per_device(query_rows, key_rows, value_rows, short_taps, long_filter, cotangent):
    length, width = query_rows.shape
    groups = long_filter.shape[1]
    blocks = lax.axis_size("seq")
    chans = lax.axis_size("chan")
    bits = []
    while 1 << len(bits) < blocks:
        bits.append(1 << len(bits))
    bits.reverse()
    forward, inverse = dft_tables(length)

    unit_shape = jax.ShapeDtypeStruct(
        (2 * length + 2 * (length * groups // width) + HALO, width), BF16
    )
    own_units = pl.pallas_call(
        functools.partial(pack_kernel, bits),
        out_shape=[unit_shape] * len(bits),
        in_specs=[VMEM] * 5,
        out_specs=[VMEM] * len(bits),
    )(query_rows, key_rows, value_rows, cotangent, long_filter)

    def swap(block, bit):
        return lax.ppermute(block, "seq", [(i, i ^ bit) for i in range(blocks)])

    units = {}
    for bit, own in zip(bits, own_units):
        arrived = {bit: swap(own, bit)}
        for index, block in units.items():
            arrived[index ^ bit] = swap(block, bit)
        units.update(arrived)
    units = [units[index] for index in range(1, blocks)]

    tile_width = min(width, 256)
    rows_out = jax.ShapeDtypeStruct((length, width), BF16)
    hyena_out, grad_query, grad_key, grad_value, partial = pl.pallas_call(
        functools.partial(main_kernel, blocks, tile_width),
        out_shape=[rows_out] * 4 + [jax.ShapeDtypeStruct((blocks, length, groups), F32)],
        in_specs=[VMEM] * (8 + blocks - 1),
        out_specs=[VMEM] * 5,
        scratch_shapes=[
            pltpu.VMEM((blocks + 2, length + 2 * EDGE, tile_width), F32),
            pltpu.VMEM((blocks + 2, length + 2 * EDGE, tile_width), F32),
            pltpu.VMEM((blocks, 2 * length, groups), F32),
            pltpu.VMEM((blocks + 3, length, groups), F32),
            pltpu.VMEM((blocks, 2 * length, groups), F32),
            pltpu.VMEM((2 * length, tile_width), F32),
            pltpu.VMEM((2, 2 * length, tile_width), F32),
            pltpu.VMEM((2 * EDGE, tile_width), F32),
            pltpu.VMEM((3, length + EDGE, tile_width), F32),
        ],
        compiler_params=pltpu.CompilerParams(vmem_limit_bytes=48 * 1024 * 1024),
    )(
        query_rows,
        key_rows,
        value_rows,
        cotangent,
        short_taps,
        long_filter,
        forward,
        inverse,
        *units,
    )

    summed = lax.all_to_all(partial, "seq", 0, 0, tiled=True).sum(axis=0)
    shares = summed.reshape(chans, length // chans, groups)
    share = lax.all_to_all(shares, "chan", 0, 0, tiled=True).sum(axis=0)
    spread = jnp.broadcast_to(share, shares.shape)
    grad_filter = lax.all_to_all(spread, "chan", 0, 0, tiled=True).reshape(length, groups)
    return (hyena_out, grad_query, grad_key, grad_value, grad_filter)


def solution(mesh):
    in_specs = (
        P("seq", "chan"),
        P("seq", "chan"),
        P("seq", "chan"),
        P(None, None, "chan"),
        P("seq", None),
        P("seq", "chan"),
    )
    out_specs = (
        P("seq", "chan"),
        P("seq", "chan"),
        P("seq", "chan"),
        P("seq", "chan"),
        P("seq", None),
    )
    return jax.shard_map(
        per_device, mesh=mesh, in_specs=in_specs, out_specs=out_specs, check_vma=False
    )
```

time: 234 us -> 66.3 us (0.28); the launches traced: 229 us -> 66 us
  waiting for transfers between devices: 73.2 us -> 16.3 us
  matrix products: 52.8 us -> 0 us
  local copies, waits for them, and re-layouts: 35.8 us -> 3.31 us
  starting transfers between devices: 35.3 us -> 2.97 us
  blocking collectives: 0 us -> 31.3 us
  other arithmetic: 17 us -> 0.03 us
  between operations: 15 us -> 0.72 us
  Pallas kernels: 0 us -> 11.3 us
    psum x1 -> x0, waiting for transfers between devices: 59.8 us -> none  [per_device(): grad_filter = lax.psum(filter_local, 'chan')]
    dot_general x24 -> x0, matrix products: 52.8 us -> none  [product(): return jnp.einsum(pattern, matrix, operand, precision=lax.Precision.HIGHEST)]
    all_to_all x0 -> x3, blocking collectives: none -> 31.3 us  [the longest x1 12.5 us: per_device(): share = lax.all_to_all(shares, 'chan', 0, 0, tiled=True).sum(axis=0)]
    all_to_all x6 -> x0, starting transfers between devices: 23.2 us -> none  [the longest x3 12.4 us: to_channels(): lax.all_to_all(values, 'seq', split_axis=1, concat_axis=0, tiled=True)]
    ppermute x6 -> x3, waiting for transfers between devices: 0.02 us -> 16.3 us  [swap(): return lax.ppermute(block, 'seq', [(i, i ^ bit) for i in range(blocks)])]
    all_to_all x6 -> x0, waiting for transfers between devices: 13.4 us -> none  [the longest x3 11.1 us: to_blocks(): lax.all_to_all(values, 'seq', split_axis=0, concat_axis=1, tiled=True)]
    pallas_call x0 -> x2, Pallas kernels: none -> 11.3 us  [the longest x1 8.88 us: per_device(): pl.pallas_call(functools.partial(main_kernel, blocks, tile_width), out_sh...]
    ppermute x6 -> x3, starting transfers between devices: 12.1 us -> 2.97 us  [swap(): return lax.ppermute(block, 'seq', [(i, i ^ bit) for i in range(blocks)])]
  transfers between devices with their start and end apart: 13 -> 3, of which waited for: 4 -> 2; matrix products, arithmetic and copies ran while one was open for 24% -> 0% of each run, Pallas kernels for 0% -> 0%
where the time goes in v1:
time: 66.3 us; the launch traced here: 66 us
  blocking collectives  31.3 us (47%)
  waiting for transfers between devices  16.3 us (25%)
  Pallas kernels  11.3 us (17%)
  local copies, waits for them, and re-layouts  3.31 us (5%)
  starting transfers between devices  2.97 us (4%)
  between operations  0.72 us (1%)
    ppermute x3, waiting for transfers between devices, swap(): return lax.ppermute(block, 'seq', [(i, i ^ bit) for i in range(blocks)])  16.3 us
    all_to_all x1, blocking collectives, per_device(): share = lax.all_to_all(shares, 'chan', 0, 0, tiled=True).sum(axis=0)  12.5 us
    all_to_all x1, blocking collectives, per_device(): summed = lax.all_to_all(partial, 'seq', 0, 0, tiled=True).sum(axis=0)  9.55 us
    all_to_all x1, blocking collectives, per_device(): lax.all_to_all(spread, 'chan', 0, 0, tiled=True).reshape(length, groups)  9.29 us
    pallas_call x1, Pallas kernels, per_device(): pl.pallas_call(functools.partial(main_kernel, blocks, tile_width), out_sh...  8.88 us
    unnamed x17, local copies, waits for them, and re-layouts  3.3 us
    ppermute x3, starting transfers between devices, swap(): return lax.ppermute(block, 'seq', [(i, i ^ bit) for i in range(blocks)])  2.97 us
    pallas_call x1, Pallas kernels, per_device(): pl.pallas_call(functools.partial(pack_kernel, bits), out_shape=[unit_shap...  2.41 us
  transfers between devices with their start and end apart: 3, of which 2 were waited for; matrix products, arithmetic and copies ran while one was open for 0% of the time, Pallas kernels for 0%

profile of v1, /device:TPU:0, one launch (start us, length us, event | category | flops | bytes accessed | tf_op | source)
XLA Modules:
  0.0 66.0 jit_solution(14726569084941304690)
XLA Ops:
  0.6 0.0 copy-start.3
  0.6 0.0 copy-start.4
  0.7 0.0 copy-start.2
  0.7 0.0 copy-start.1
  0.7 0.0 copy-start
  0.7 2.4 %shard_map.119 = (bf16[304,1024]{1,0:T(8,128)(2,1)}, bf16[304,1024]{1,0:T(8,128)(2,1)}) custom-call(bf16[128,1024]{1,0:T(8,128)(2,1)} %q_ref.3, bf16[128,1024]{1,0:T(8,128)(2,1)} %k_ref.3, bf16[128,1024]{1,0:T(8,128)(2,1)} %v_ref.3, bf16[128,1024]{1,0:T(8,128)(2,1)} %c_ref.3, f32[128,128]{1,0:T(8,128)} %filter_ref.3), custom_call_target="tpu_custom_call" | custom-call | tf_op jit(solution)/shard_map/pallas_call | solution.py:319
  3.1 3.0 %collective-permute-start.1 = (bf16[304,1024]{1,0:T(8,128)(2,1)}, bf16[304,1024]{1,0:T(8,128)(2,1)S(1)}, u32[]{:S(2)}, u32[]{:S(2)}) collective-permute-start(bf16[304,1024]{1,0:T(8,128)(2,1)} %get-tuple-element.13), channel_id=1, source_target_pairs={{0,16},{8,24},{16,0},{24,8},{1,17},{9,25},{17,1},{25,9},{2,18},{10... | collective-permute-start | bytes 1867784 | tf_op jit(solution)/shard_map/ppermute | solution.py:327
  6.1 0.0 collective-permute-start
  6.1 14.2 %collective-permute-done.1.refs_1_ = bf16[304,1024]{1,0:T(8,128)(2,1)S(1)} collective-permute-done((bf16[304,1024]{1,0:T(8,128)(2,1)}, bf16[304,1024]{1,0:T(8,128)(2,1)S(1)}, u32[]{:S(2)}, u32[]{:S(2)}) %collective-permute-start.1) | collective-permute-done | bytes 622624 | tf_op jit(solution)/shard_map/ppermute | solution.py:327
  20.3 0.0 collective-permute-start.2
  20.3 0.0 collective-permute-done.refs_0_
  20.3 2.0 %collective-permute-done.2.refs_2_ = bf16[304,1024]{1,0:T(8,128)(2,1)S(1)} collective-permute-done((bf16[304,1024]{1,0:T(8,128)(2,1)S(1)}, bf16[304,1024]{1,0:T(8,128)(2,1)S(1)}, u32[]{:S(2)}, u32[]{:S(2)}) %collective-permute-start.2) | collective-permute-done | bytes 622624 | tf_op jit(solution)/shard_map/ppermute | solution.py:327
  22.4 0.0 copy-done.3
  22.4 0.0 copy-done.4
  22.4 0.0 copy-done.2
  22.4 0.0 copy-start.5
  22.4 0.9 %copy-done.5 = bf16[136,768]{1,0:T(8,128)(2,1)S(1)} copy-done((bf16[136,768]{1,0:T(8,128)(2,1)S(1)}, bf16[136,768]{1,0:T(8,128)(2,1)}, u32[]{:S(2)}) %copy-start.5) | copy-done | bytes 208920
  23.3 0.9 %copy-done.6 = bf16[256,384]{1,0:T(8,128)(2,1)S(1)} copy-done((bf16[256,384]{1,0:T(8,128)(2,1)S(1)}, bf16[256,384]{1,0:T(8,128)(2,1)}, u32[]{:S(2)}) %copy-start.6) | copy-done | bytes 196632
  24.2 0.8 %copy-done.7 = f32[3,3,1024]{2,1,0:T(4,128)S(1)} copy-done((f32[3,3,1024]{2,1,0:T(4,128)S(1)}, f32[3,3,1024]{2,1,0:T(4,128)}, u32[]{:S(2)}) %copy-start.7) | copy-done | bytes 36888
  25.0 8.9 %shard_map.120 = (bf16[128,1024]{1,0:T(8,128)(2,1)}, bf16[128,1024]{1,0:T(8,128)(2,1)}, bf16[128,1024]{1,0:T(8,128)(2,1)}, bf16[128,1024]{1,0:T(8,128)(2,1)}, f32[4,128,128]{2,1,0:T(8,128)S(1)}) custom-call(bf16[128,1024]{1,0:T(8,128)(2,1)S(1)} %copy-done, bf16[128,1024]{1,0:T(8,128)(2,1)S(1)} %copy-done.1, bf16[128,1024]{1,0:T(8,128)(2,1)S(1)} %copy-done.2, ...), custom_call_target="tpu_custom_call" | custom-call | tf_op jit(solution)/shard_map/pallas_call | solution.py:339
  33.9 9.6 %all_to_all.15 = f32[4,128,128]{2,1,0:T(8,128)S(1)} all-to-all(f32[4,128,128]{2,1,0:T(8,128)S(1)} %get-tuple-element.18), channel_id=1, replica_groups=mesh['seq'=4,'chan'=8] {'seq'}, dimensions={0} | all-to-all | bytes 524288 | tf_op jit(solution)/shard_map/all_to_all | solution.py:368
  43.5 12.5 %all_to_all.16 = f32[8,16,128]{2,1,0:T(8,128)S(1)} all-to-all(f32[8,16,128]{2,1,0:T(8,128)S(1)} %bitcast.2), channel_id=1, replica_groups=mesh['seq'=4,'chan'=8] {'chan'}, dimensions={0} | all-to-all | bytes 131072 | tf_op jit(solution)/shard_map/all_to_all | solution.py:370
  56.0 9.3 %all_to_all.17 = f32[8,16,128]{2,1,0:T(8,128)S(1)} all-to-all(f32[8,16,128]{2,1,0:T(8,128)S(1)} %broadcast_in_dim.3), channel_id=1, replica_groups=mesh['seq'=4,'chan'=8] {'chan'}, dimensions={0} | all-to-all | bytes 131072 | tf_op jit(solution)/shard_map/all_to_all | solution.py:372
  65.3 0.6 copy.14
  (7 shorter events, 0.0 us)
Async XLA Ops:
  0.6 21.7 %copy-start.3 = (bf16[128,1024]{1,0:T(8,128)(2,1)S(1)}, bf16[128,1024]{1,0:T(8,128)(2,1)}, u32[]{:S(2)}) copy-start(bf16[128,1024]{1,0:T(8,128)(2,1)} %c_ref.3) | copy-start | bytes 786436
  0.6 21.7 %copy-start.4 = (f32[128,128]{1,0:T(8,128)S(1)}, f32[128,128]{1,0:T(8,128)}, u32[]{:S(2)}) copy-start(f32[128,128]{1,0:T(8,128)} %filter_ref.3) | copy-start | bytes 196612
  0.7 21.7 %copy-start.2 = (bf16[128,1024]{1,0:T(8,128)(2,1)S(1)}, bf16[128,1024]{1,0:T(8,128)(2,1)}, u32[]{:S(2)}) copy-start(bf16[128,1024]{1,0:T(8,128)(2,1)} %v_ref.3) | copy-start | bytes 786436
  0.7 21.7 %copy-start.1 = (bf16[128,1024]{1,0:T(8,128)(2,1)S(1)}, bf16[128,1024]{1,0:T(8,128)(2,1)}, u32[]{:S(2)}) copy-start(bf16[128,1024]{1,0:T(8,128)(2,1)} %k_ref.3) | copy-start | bytes 786436
  0.7 21.7 %copy-start = (bf16[128,1024]{1,0:T(8,128)(2,1)S(1)}, bf16[128,1024]{1,0:T(8,128)(2,1)}, u32[]{:S(2)}) copy-start(bf16[128,1024]{1,0:T(8,128)(2,1)} %q_ref.3) | copy-start | bytes 786436
  3.1 17.2 %collective-permute-start.1 = (bf16[304,1024]{1,0:T(8,128)(2,1)}, bf16[304,1024]{1,0:T(8,128)(2,1)S(1)}, u32[]{:S(2)}, u32[]{:S(2)}) collective-permute-start(bf16[304,1024]{1,0:T(8,128)(2,1)} %get-tuple-element.13), channel_id=1, source_target_pairs={{0,16},{8,24},{16,0},{24,8},{1,17},{9,25},{17,1},{25,9},{2,18},{10... | collective-permute-start | bytes 1867784 | tf_op jit(solution)/shard_map/ppermute | solution.py:327
  6.1 14.2 %collective-permute-start = (bf16[304,1024]{1,0:T(8,128)(2,1)}, bf16[304,1024]{1,0:T(8,128)(2,1)S(1)}, u32[]{:S(2)}, u32[]{:S(2)}) collective-permute-start(bf16[304,1024]{1,0:T(8,128)(2,1)} %get-tuple-element.12), channel_id=1, source_target_pairs={{0,8},{8,0},{16,24},{24,16},{1,9},{9,1},{17,25},{25,17},{2,10},{10... | collective-permute-start | bytes 1867784 | tf_op jit(solution)/shard_map/ppermute | solution.py:327
  20.3 2.1 %collective-permute-start.2 = (bf16[304,1024]{1,0:T(8,128)(2,1)S(1)}, bf16[304,1024]{1,0:T(8,128)(2,1)S(1)}, u32[]{:S(2)}, u32[]{:S(2)}) collective-permute-start(bf16[304,1024]{1,0:T(8,128)(2,1)S(1)} %collective-permute-done.1.refs_1_), channel_id=1, source_target_pairs={{0,8},{8,0},{16,24},{24,16},{1,9},{9,1},{17,25},{25,17},{2,10},{10... | collective-permute-start | bytes 1867784 | tf_op jit(solution)/shard_map/ppermute | solution.py:327
  22.4 0.9 %copy-start.5 = (bf16[136,768]{1,0:T(8,128)(2,1)S(1)}, bf16[136,768]{1,0:T(8,128)(2,1)}, u32[]{:S(2)}) copy-start(bf16[136,768]{1,0:T(8,128)(2,1)} %constant.7.clone.inverse_ref) | copy-start | bytes 626692
  23.3 0.9 %copy-start.6 = (bf16[256,384]{1,0:T(8,128)(2,1)S(1)}, bf16[256,384]{1,0:T(8,128)(2,1)}, u32[]{:S(2)}) copy-start(bf16[256,384]{1,0:T(8,128)(2,1)} %constant.6.clone.forward_ref) | copy-start | bytes 589828
  24.2 0.8 %copy-start.7 = (f32[3,3,1024]{2,1,0:T(4,128)S(1)}, f32[3,3,1024]{2,1,0:T(4,128)}, u32[]{:S(2)}) copy-start(f32[3,3,1024]{2,1,0:T(4,128)} %taps_ref.1) | copy-start | bytes 110596
